TPU v7x, 32 devices: a whole 2x2x4 slice. The times are simulated.
32 devices in a mesh: grp: 4 (over x, core), sub: 8 (over z, y).
Axes of the slice: x: 2, y: 2, z: 4, core: 2. Of those that a mesh axis runs over, the one named last changes fastest.
Arguments:
- operators: float32 [4, 8, 4, 512, 512], P('grp', 'sub'), may hold values from -1 to 6
- counts: int32 [4, 8], P('grp', 'sub'), may hold values from 1 to 4, as said below
- pair_rows: int32 [4, 8, 4, 256], P('grp', 'sub'), may hold values from -256 to 256, as said below
- gap: float32 [4, 8, 4, 256, 128], P('grp', 'sub'), may hold values from -6 to 6
Outputs:
- multipliers: float32 [4, 8, 4, 256, 128], P('grp', 'sub')
- residual: float32 [4, 8, 4, 256, 128], P('grp', 'sub')
Inputs may be any that keep to these rules, and one draw needn't show every extreme that they name: `counts`: each group has at least one owner with 4 subdomains. `pair_rows`: for each group, owner and slot the absolute values are a permutation of 1 to 256.
All inputs are finite; a program needn't handle non-finite values.
Results may differ from a plain program's by a relative error of at most 0.00022.
Values sent between devices are 32-bit elements; how exact they have to be, the bound alone decides.
No kernel may reach another device: no remote copies, remote signals or barrier semaphores. Data moves between devices by JAX's collectives and lax.ppermute only.
A program may use at most 64 MiB of HBM per device.

v0:
```python
import functools

import jax
import jax.numpy as jnp
from jax import lax
from jax.experimental import pallas as pl
from jax.experimental.pallas import tpu as pltpu
from jax.sharding import PartitionSpec as P

ITERS = 6
LOWER = 1.0
UPPER = 14.0
CENTRE = (UPPER + LOWER) / 2.0
RADIUS = (UPPER - LOWER) / 2.0
BF16 = jnp.bfloat16
F32 = jnp.float32
VMEM_BYTES = 24 * 1024 * 1024


def chebyshev_factors():
    spread = CENTRE / RADIUS
    rho = 1.0 / spread
    factors = []
    for _ in range(ITERS - 1):
        rho_new = 1.0 / (2.0 * spread - rho)
        factors.append((rho_new * rho, 2.0 * rho_new / RADIUS))
        rho = rho_new
    return factors


def pairings(groups, owners):
    found = []
    for first in (0, 1):
        route = []
        for g in range(groups):
            for s in range(owners):
                t = s + 1 if (s - first) % 2 == 0 else s - 1
                h = g
                if t < 0 or t >= owners:
                    t = s
                    h = g ^ 1
                if h < groups:
                    route.append((g * owners + s, h * owners + t))
        found.append(route)
    return found


def halves(x):
    high = x.astype(BF16)
    return high, (x - high.astype(F32)).astype(BF16)


def beside(x):
    both = jnp.concatenate(halves(x), axis=1)
    return jnp.concatenate([both, both], axis=0)


def split_dot(matrix, cases):
    wide = jnp.dot(matrix, cases, preferred_element_type=F32)
    width = wide.shape[1] // 2
    return wide[:, :width] + wide[:, width:]


def dot_nt(a, b):
    return lax.dot_general(a, b, (((1,), (1,)), ((), ())), preferred_element_type=F32)


def signed_placement(pairs):
    h = pairs.shape[1]
    rows = lax.broadcasted_iota(jnp.int32, (h, h), 0)
    picked = jnp.abs(pairs) - 1
    sign = jnp.where(pairs > 0, 1.0, -1.0)
    return jnp.where(rows == picked, sign, 0.0).astype(BF16)


def exists_of(count, pos, owners, slot):
    there = jnp.logical_and(slot < count, jnp.logical_or(pos < owners - 1, slot != count - 1))
    return jnp.where(there, 1.0, 0.0)


def first_kernel(owners, info, operators, pairs, gap, left_out, image_out, even_out, odd_out, direction, top, sem):
    count, pos = info[0], info[1]
    slots, h = gap.shape[0], gap.shape[1]
    copy = pltpu.make_async_copy(operators.at[0, 0, 0, pl.ds(0, h)], top, sem)
    copy.start()
    for j in range(slots):
        image_out[j] = gap[j] * exists_of(count, pos, owners, j)
        direction[j] = image_out[j] / CENTRE
    place = signed_placement(pairs[pl.ds(0, 1), :])
    copy.wait()
    high, low = halves(top[...])
    placed = [jnp.dot(place, part, preferred_element_type=F32).astype(BF16) for part in (high, low)]
    square = [dot_nt(part[:, :h], place) for part in placed]
    left_out[...] = square[0] + square[1]
    across = jnp.concatenate([-part[:, h:] for part in placed], axis=1)
    behind = split_dot(across, beside(direction[0]))
    send(pos, direction[count - 1], behind, even_out, odd_out)


def send(pos, ahead, behind, even_out, odd_out):
    is_even = lax.rem(pos, 2) == 0

    @pl.when(is_even)
    def _():
        even_out[...] = ahead
        odd_out[...] = behind

    @pl.when(jnp.logical_not(is_even))
    def _():
        even_out[...] = behind
        odd_out[...] = ahead


def operator_kernel(info, operators, pairs, own_out, lower_out, upper_out, whole, sems):
    count = info[0]
    slots, h = pairs.shape
    copies = [pltpu.make_async_copy(operators.at[0, 0, j], whole.at[j], sems.at[j]) for j in range(slots)]
    for copy in copies:
        copy.start()
    for j in range(slots):
        copies[j].wait()
        place = signed_placement(pairs[pl.ds(j, 1), :])
        squares = []
        for k, part in enumerate(halves(whole[j])):
            columns = pl.ds(k * h, h)
            placed = jnp.dot(place, part[:h], preferred_element_type=F32).astype(BF16)
            upper_out[j, :, columns] = -placed[:, h:]
            turned = dot_nt(jnp.concatenate([placed[:, :h], part[h:, :h]], axis=0), place)
            squares.append(turned[:h])
            lower_out[j, :, columns] = -turned[h:].astype(BF16)
        if j > 0:
            added = jnp.where(j < count, squares[0] + squares[1], 0.0)
            high, low = halves(whole[j - 1, pl.ds(h, h), pl.ds(h, h)] + added)
            own_out[j - 1, :, pl.ds(0, h)] = high
            own_out[j - 1, :, pl.ds(h, h)] = low
    high, low = halves(whole[slots - 1, pl.ds(h, h), pl.ds(h, h)])
    own_out[slots - 1, :, pl.ds(0, h)] = high
    own_out[slots - 1, :, pl.ds(h, h)] = low


def join_kernel(info, own, left, own_out):
    last = info[0] - 1
    h = left.shape[0]
    total = own[last, :, pl.ds(0, h)].astype(F32) + own[last, :, pl.ds(h, h)].astype(F32) + left[...]
    high, low = halves(total)
    own_out[last, :, pl.ds(0, h)] = high
    own_out[last, :, pl.ds(h, h)] = low


def inner_kernel(owners, started, info, own, lower, upper, direction, residual, total, residual_out, total_out):
    count, pos = info[0], info[1]
    slots = direction.shape[0]
    cases = [beside(direction[j]) for j in range(slots)]
    for j in range(slots):
        image = split_dot(own[j], cases[j])
        if j > 0:
            image += split_dot(lower[j], cases[j - 1])
        if j + 1 < slots:
            image += split_dot(upper[j + 1], cases[j + 1])
        residual_out[j] = residual[j] - image * exists_of(count, pos, owners, j)
        total_out[j] = total[j] + direction[j] if started else direction[j]


def received(pos, even_in, odd_in):
    is_even = lax.rem(pos, 2) == 0
    before = jnp.where(is_even, odd_in[...], even_in[...])
    behind = jnp.where(is_even, even_in[...], odd_in[...])
    return jnp.where(pos > 0, before, 0.0), behind


def finish_residual(owners, info, lower, even_in, odd_in, residual, residual_out):
    count, pos = info[0], info[1]
    slots = residual.shape[0]
    before, behind = received(pos, even_in, odd_in)
    for j in range(slots):
        residual_out[j] = residual[j]
    residual_out[0] -= split_dot(lower[0], beside(before)) * exists_of(count, pos, owners, 0)
    last = count - 1
    residual_out[last] -= behind * exists_of(count, pos, owners, last)


def edge_kernel(owners, factors, info, lower, upper, even_in, odd_in, direction, residual, residual_out, direction_out, even_out, odd_out):
    count, pos = info[0], info[1]
    finish_residual(owners, info, lower, even_in, odd_in, residual, residual_out)
    for j in range(direction.shape[0]):
        direction_out[j] = factors[0] * direction[j] + factors[1] * residual_out[j]
    behind = split_dot(upper[0], beside(direction_out[0]))
    send(pos, direction_out[count - 1], behind, even_out, odd_out)


def last_kernel(owners, info, lower, even_in, odd_in, residual, residual_out):
    finish_residual(owners, info, lower, even_in, odd_in, residual, residual_out)


SMEM = pl.BlockSpec(memory_space=pltpu.SMEM)
VMEM = pl.BlockSpec(memory_space=pltpu.VMEM)
ANY = pl.BlockSpec(memory_space=pl.ANY)


def call(kernel, ins, outs, name, scratch=(), aliases=None, flops=0):
    return pl.pallas_call(
        kernel,
        in_specs=ins,
        out_specs=[VMEM] * len(outs),
        out_shape=[jax.ShapeDtypeStruct(shape, kind) for shape, kind in outs],
        scratch_shapes=list(scratch),
        input_output_aliases=aliases or {},
        compiler_params=pltpu.CompilerParams(vmem_limit_bytes=VMEM_BYTES),
        cost_estimate=pl.CostEstimate(flops=flops, bytes_accessed=1000000, transcendentals=0),
        name=name,
    )


def shards(groups, owners, operators, counts, pair_rows, gap):
    pairs, source = pair_rows[0, 0], gap[0, 0]
    slots, h, cases = source.shape
    m = operators.shape[-1]
    pos = lax.axis_index("sub").astype(jnp.int32)
    info = jnp.stack([counts[0, 0], pos])
    evens, odds = pairings(groups, owners)
    ring = [((s + 1) % owners, s) for s in range(owners)]
    field = ((slots, h, cases), F32)
    block = ((h, cases), F32)
    matrices = ((slots, h, 2 * h), BF16)

    def exchange(even, odd):
        odd = lax.ppermute(odd, ("grp", "sub"), odds)
        even = lax.ppermute(even, ("grp", "sub"), evens)
        return even, odd

    left, residual, even, odd, direction = call(
        functools.partial(first_kernel, owners),
        [SMEM, ANY, VMEM, VMEM],
        [((h, h), F32), field, block, block, field],
        "first_messages",
        [pltpu.VMEM((h, m), F32), pltpu.SemaphoreType.DMA],
    )(info, operators, pairs, source)
    even, odd = exchange(even, odd)
    left = lax.ppermute(left, "sub", ring)
    own, lower, upper = call(
        operator_kernel,
        [SMEM, ANY, VMEM],
        [matrices] * 3,
        "block_operators",
        [pltpu.VMEM((slots, m, m), F32), pltpu.SemaphoreType.DMA((slots,))],
    )(info, operators, pairs)
    (own,) = call(join_kernel, [SMEM, VMEM, VMEM], [matrices], "join_left", aliases={1: 0})(info, own, left)
    total = direction
    for step, factors in enumerate(chebyshev_factors() + [None]):
        residual, total = call(
            functools.partial(inner_kernel, owners, step > 0),
            [SMEM] + [VMEM] * 6,
            [field, field],
            "inner_blocks",
            flops=20 * h * h * cases * 4,
        )(info, own, lower, upper, direction, residual, total)
        if factors is None:
            (residual,) = call(
                functools.partial(last_kernel, owners), [SMEM] + [VMEM] * 4, [field], "last_residual"
            )(info, lower, even, odd, residual)
        else:
            residual, direction, even, odd = call(
                functools.partial(edge_kernel, owners, factors),
                [SMEM] + [VMEM] * 6,
                [field, field, block, block],
                "edge_blocks",
            )(info, lower, upper, even, odd, direction, residual)
            even, odd = exchange(even, odd)
    return total[None, None], residual[None, None]


def solution(mesh):
    groups, owners = mesh.shape["grp"], mesh.shape["sub"]
    return jax.shard_map(
        functools.partial(shards, groups, owners),
        mesh=mesh,
        in_specs=(
            P("grp", "sub", None, None, None),
            P("grp", "sub"),
            P("grp", "sub", None, None),
            P("grp", "sub", None, None, None),
        ),
        out_specs=(P("grp", "sub", None, None, None), P("grp", "sub", None, None, None)),
        check_vma=False,
    )
```

profile of v0, /device:TPU:0, one launch (start us, length us, event | category | flops | bytes accessed | tf_op | source)
XLA Modules:
  0.0 65.4 jit_solution(15792979344238186970)
XLA Ops:
  1.3 0.1 pad_add_fusion.info
  1.4 0.0 copy-start
  1.4 2.2 %copy-done = f32[1,1,4,512,512]{4,3,2,1,0:T(8,128)S(1)} copy-done((f32[1,1,4,512,512]{4,3,2,1,0:T(8,128)S(1)}, f32[1,1,4,512,512]{4,3,2,1,0:T(8,128)}, u32[]{:S(2)}) %copy-start) | copy-done | bytes 4194328
  3.5 0.0 copy-start.1
  3.5 1.0 %copy-done.1 = f32[1,1,4,256,128]{4,3,2,1,0:T(8,128)S(1)} copy-done((f32[1,1,4,256,128]{4,3,2,1,0:T(8,128)S(1)}, f32[1,1,4,256,128]{4,3,2,1,0:T(8,128)}, u32[]{:S(2)}) %copy-start.1) | copy-done | bytes 524312
  4.6 0.0 copy-start.2
  4.6 0.7 %copy-done.2 = s32[1,1,4,256]{3,2,1,0:T(4,128)S(1)} copy-done((s32[1,1,4,256]{3,2,1,0:T(4,128)S(1)}, s32[1,1,4,256]{3,2,1,0:T(4,128)}, u32[]{:S(2)}) %copy-start.2) | copy-done | bytes 4120
  5.3 1.2 %first_messages.1 = (f32[256,256]{1,0:T(8,128)S(1)}, f32[4,256,128]{2,1,0:T(8,128)S(1)}, f32[256,128]{1,0:T(8,128)S(1)}, f32[256,128]{1,0:T(8,128)S(1)}, f32[4,256,128]{2,1,0:T(8,128)S(1)}) custom-call(s32[2]{0:T(128)S(1)} %pad_add_fusion.info, f32[1,1,4,512,512]{4,3,2,1,0:T(8,128)S(1)} %copy-done, s32[4,256]{1,0:T(4,128)S(1)} %bitcast.8, ...), custom_call_target="tpu_custom_call" | custom-call | bytes 1000000 | tf_op jit(solution)/shard_map/first_messages/pallas_call | solution.py:231
  6.5 6.1 %collective-permute-start = (f32[256,256]{1,0:T(8,128)S(1)}, f32[256,256]{1,0:T(8,128)S(1)}, u32[]{:S(2)}, u32[]{:S(2)}) collective-permute-start(f32[256,256]{1,0:T(8,128)S(1)} %get-tuple-element.43), channel_id=1, source_target_pairs={{1,0},{2,1},{3,2},{4,3},{5,4},{6,5},{7,6},{0,7},{9,8},{10,9},{11,1... | collective-permute-start | bytes 786440 | tf_op jit(solution)/shard_map/ppermute | solution.py:239
  12.6 0.0 collective-permute-start.1
  12.6 0.0 collective-permute-start.2
  12.6 3.1 %block_operators.1 = (bf16[4,256,512]{2,1,0:T(8,128)(2,1)S(1)}, bf16[4,256,512]{2,1,0:T(8,128)(2,1)S(1)}, bf16[4,256,512]{2,1,0:T(8,128)(2,1)S(1)}) custom-call(s32[2]{0:T(128)S(1)} %pad_add_fusion.info, f32[1,1,4,512,512]{4,3,2,1,0:T(8,128)S(1)} %copy-done, s32[4,256]{1,0:T(4,128)S(1)} %bitcast.9), custom_call_target="tpu_custom_call" | custom-call | bytes 1000000 | tf_op jit(solution)/shard_map/block_operators/pallas_call | solution.py:240
  15.7 2.4 %collective-permute-done.left = f32[256,256]{1,0:T(8,128)S(1)} collective-permute-done((f32[256,256]{1,0:T(8,128)S(1)}, f32[256,256]{1,0:T(8,128)S(1)}, u32[]{:S(2)}, u32[]{:S(2)}) %collective-permute-start) | collective-permute-done | bytes 262176 | tf_op jit(solution)/shard_map/ppermute | solution.py:239
  18.1 0.6 join_left.1.own
  18.7 1.4 %inner_blocks.6 = (f32[4,256,128]{2,1,0:T(8,128)S(1)}, f32[4,256,128]{2,1,0:T(8,128)S(1)}) custom-call(s32[2]{0:T(128)S(1)} %pad_add_fusion.info, bf16[4,256,512]{2,1,0:T(8,128)(2,1)S(1)} %join_left.1.own, bf16[4,256,512]{2,1,0:T(8,128)(2,1)S(1)} %get-tuple-element.44.lower, bf16[4,256,512]{2,1,0:T(8,128)(2,1)S(1)} %get-tuple-element.45.upper, ...), custom_call_target="tpu_custom_call" | custom-call | flops 671088640 | bytes 1000000 | tf_op jit(solution)/shard_map/inner_blocks/pallas_call | solution.py:250
  20.2 1.4 %collective-permute-done.1.even_in = f32[256,128]{1,0:T(8,128)S(1)} collective-permute-done((f32[256,128]{1,0:T(8,128)S(1)}, f32[256,128]{1,0:T(8,128)S(1)}, u32[]{:S(2)}, u32[]{:S(2)}) %collective-permute-start.1) | collective-permute-done | bytes 131104 | tf_op jit(solution)/shard_map/ppermute | solution.py:228
  21.6 0.0 collective-permute-done.2.odd_in
  21.6 1.2 %edge_blocks.5 = (f32[4,256,128]{2,1,0:T(8,128)S(1)}, f32[4,256,128]{2,1,0:T(8,128)S(1)}, f32[256,128]{1,0:T(8,128)S(1)}, f32[256,128]{1,0:T(8,128)S(1)}) custom-call(s32[2]{0:T(128)S(1)} %pad_add_fusion.info, bf16[4,256,512]{2,1,0:T(8,128)(2,1)S(1)} %get-tuple-element.44.lower, bf16[4,256,512]{2,1,0:T(8,128)(2,1)S(1)} %get-tuple-element.45.upper, ...), custom_call_target="tpu_custom_call" | custom-call | bytes 1000000 | tf_op jit(solution)/shard_map/edge_blocks/pallas_call | solution.py:262
  22.8 2.6 %collective-permute-start.3 = (f32[256,128]{1,0:T(8,128)S(1)}, f32[256,128]{1,0:T(8,128)S(1)}, u32[]{:S(2)}, u32[]{:S(2)}) collective-permute-start(f32[256,128]{1,0:T(8,128)S(1)} %get-tuple-element.51), channel_id=1, source_target_pairs={{0,1},{1,0},{2,3},{3,2},{4,5},{5,4},{6,7},{7,6},{8,9},{9,8},{10,11... | collective-permute-start | bytes 393224 | tf_op jit(solution)/shard_map/ppermute | solution.py:228
  25.4 0.0 collective-permute-start.4
  25.4 1.4 %inner_blocks.7 = (f32[4,256,128]{2,1,0:T(8,128)S(1)}, f32[4,256,128]{2,1,0:T(8,128)S(1)}) custom-call(s32[2]{0:T(128)S(1)} %pad_add_fusion.info, bf16[4,256,512]{2,1,0:T(8,128)(2,1)S(1)} %join_left.1.own, bf16[4,256,512]{2,1,0:T(8,128)(2,1)S(1)} %get-tuple-element.44.lower, bf16[4,256,512]{2,1,0:T(8,128)(2,1)S(1)} %get-tuple-element.45.upper, ...), custom_call_target="tpu_custom_call" | custom-call | flops 671088640 | bytes 1000000 | tf_op jit(solution)/shard_map/inner_blocks/pallas_call | solution.py:250
  26.8 4.3 %collective-permute-done.3.even_in = f32[256,128]{1,0:T(8,128)S(1)} collective-permute-done((f32[256,128]{1,0:T(8,128)S(1)}, f32[256,128]{1,0:T(8,128)S(1)}, u32[]{:S(2)}, u32[]{:S(2)}) %collective-permute-start.3) | collective-permute-done | bytes 131104 | tf_op jit(solution)/shard_map/ppermute | solution.py:228
  31.2 0.0 collective-permute-done.4.odd_in
  31.2 1.2 %edge_blocks.6 = (f32[4,256,128]{2,1,0:T(8,128)S(1)}, f32[4,256,128]{2,1,0:T(8,128)S(1)}, f32[256,128]{1,0:T(8,128)S(1)}, f32[256,128]{1,0:T(8,128)S(1)}) custom-call(s32[2]{0:T(128)S(1)} %pad_add_fusion.info, bf16[4,256,512]{2,1,0:T(8,128)(2,1)S(1)} %get-tuple-element.44.lower, bf16[4,256,512]{2,1,0:T(8,128)(2,1)S(1)} %get-tuple-element.45.upper, ...), custom_call_target="tpu_custom_call" | custom-call | bytes 1000000 | tf_op jit(solution)/shard_map/edge_blocks/pallas_call | solution.py:262
  32.4 2.6 %collective-permute-start.5 = (f32[256,128]{1,0:T(8,128)S(1)}, f32[256,128]{1,0:T(8,128)S(1)}, u32[]{:S(2)}, u32[]{:S(2)}) collective-permute-start(f32[256,128]{1,0:T(8,128)S(1)} %get-tuple-element.57), channel_id=1, source_target_pairs={{0,1},{1,0},{2,3},{3,2},{4,5},{5,4},{6,7},{7,6},{8,9},{9,8},{10,11... | collective-permute-start | bytes 393224 | tf_op jit(solution)/shard_map/ppermute | solution.py:228
  35.0 0.0 collective-permute-start.6
  35.0 1.4 %inner_blocks.8 = (f32[4,256,128]{2,1,0:T(8,128)S(1)}, f32[4,256,128]{2,1,0:T(8,128)S(1)}) custom-call(s32[2]{0:T(128)S(1)} %pad_add_fusion.info, bf16[4,256,512]{2,1,0:T(8,128)(2,1)S(1)} %join_left.1.own, bf16[4,256,512]{2,1,0:T(8,128)(2,1)S(1)} %get-tuple-element.44.lower, bf16[4,256,512]{2,1,0:T(8,128)(2,1)S(1)} %get-tuple-element.45.upper, ...), custom_call_target="tpu_custom_call" | custom-call | flops 671088640 | bytes 1000000 | tf_op jit(solution)/shard_map/inner_blocks/pallas_call | solution.py:250
  36.4 3.5 %collective-permute-done.5.even_in = f32[256,128]{1,0:T(8,128)S(1)} collective-permute-done((f32[256,128]{1,0:T(8,128)S(1)}, f32[256,128]{1,0:T(8,128)S(1)}, u32[]{:S(2)}, u32[]{:S(2)}) %collective-permute-start.5) | collective-permute-done | bytes 131104 | tf_op jit(solution)/shard_map/ppermute | solution.py:228
  39.9 0.0 collective-permute-done.6.odd_in
  39.9 1.2 %edge_blocks.7 = (f32[4,256,128]{2,1,0:T(8,128)S(1)}, f32[4,256,128]{2,1,0:T(8,128)S(1)}, f32[256,128]{1,0:T(8,128)S(1)}, f32[256,128]{1,0:T(8,128)S(1)}) custom-call(s32[2]{0:T(128)S(1)} %pad_add_fusion.info, bf16[4,256,512]{2,1,0:T(8,128)(2,1)S(1)} %get-tuple-element.44.lower, bf16[4,256,512]{2,1,0:T(8,128)(2,1)S(1)} %get-tuple-element.45.upper, ...), custom_call_target="tpu_custom_call" | custom-call | bytes 1000000 | tf_op jit(solution)/shard_map/edge_blocks/pallas_call | solution.py:262
  41.1 2.6 %collective-permute-start.7 = (f32[256,128]{1,0:T(8,128)S(1)}, f32[256,128]{1,0:T(8,128)S(1)}, u32[]{:S(2)}, u32[]{:S(2)}) collective-permute-start(f32[256,128]{1,0:T(8,128)S(1)} %get-tuple-element.63), channel_id=1, source_target_pairs={{0,1},{1,0},{2,3},{3,2},{4,5},{5,4},{6,7},{7,6},{8,9},{9,8},{10,11... | collective-permute-start | bytes 393224 | tf_op jit(solution)/shard_map/ppermute | solution.py:228
  43.7 0.0 collective-permute-start.8
  43.7 1.4 %inner_blocks.9 = (f32[4,256,128]{2,1,0:T(8,128)S(1)}, f32[4,256,128]{2,1,0:T(8,128)S(1)}) custom-call(s32[2]{0:T(128)S(1)} %pad_add_fusion.info, bf16[4,256,512]{2,1,0:T(8,128)(2,1)S(1)} %join_left.1.own, bf16[4,256,512]{2,1,0:T(8,128)(2,1)S(1)} %get-tuple-element.44.lower, bf16[4,256,512]{2,1,0:T(8,128)(2,1)S(1)} %get-tuple-element.45.upper, ...), custom_call_target="tpu_custom_call" | custom-call | flops 671088640 | bytes 1000000 | tf_op jit(solution)/shard_map/inner_blocks/pallas_call | solution.py:250
  45.1 3.3 %collective-permute-done.7.even_in = f32[256,128]{1,0:T(8,128)S(1)} collective-permute-done((f32[256,128]{1,0:T(8,128)S(1)}, f32[256,128]{1,0:T(8,128)S(1)}, u32[]{:S(2)}, u32[]{:S(2)}) %collective-permute-start.7) | collective-permute-done | bytes 131104 | tf_op jit(solution)/shard_map/ppermute | solution.py:228
  48.4 0.0 collective-permute-done.8.odd_in
  48.4 1.2 %edge_blocks.8 = (f32[4,256,128]{2,1,0:T(8,128)S(1)}, f32[4,256,128]{2,1,0:T(8,128)S(1)}, f32[256,128]{1,0:T(8,128)S(1)}, f32[256,128]{1,0:T(8,128)S(1)}) custom-call(s32[2]{0:T(128)S(1)} %pad_add_fusion.info, bf16[4,256,512]{2,1,0:T(8,128)(2,1)S(1)} %get-tuple-element.44.lower, bf16[4,256,512]{2,1,0:T(8,128)(2,1)S(1)} %get-tuple-element.45.upper, ...), custom_call_target="tpu_custom_call" | custom-call | bytes 1000000 | tf_op jit(solution)/shard_map/edge_blocks/pallas_call | solution.py:262
  49.6 2.6 %collective-permute-start.9 = (f32[256,128]{1,0:T(8,128)S(1)}, f32[256,128]{1,0:T(8,128)S(1)}, u32[]{:S(2)}, u32[]{:S(2)}) collective-permute-start(f32[256,128]{1,0:T(8,128)S(1)} %get-tuple-element.69), channel_id=1, source_target_pairs={{0,1},{1,0},{2,3},{3,2},{4,5},{5,4},{6,7},{7,6},{8,9},{9,8},{10,11... | collective-permute-start | bytes 393224 | tf_op jit(solution)/shard_map/ppermute | solution.py:228
  52.2 0.0 collective-permute-start.10
  52.2 1.4 %inner_blocks.10 = (f32[4,256,128]{2,1,0:T(8,128)S(1)}, f32[4,256,128]{2,1,0:T(8,128)S(1)}) custom-call(s32[2]{0:T(128)S(1)} %pad_add_fusion.info, bf16[4,256,512]{2,1,0:T(8,128)(2,1)S(1)} %join_left.1.own, bf16[4,256,512]{2,1,0:T(8,128)(2,1)S(1)} %get-tuple-element.44.lower, bf16[4,256,512]{2,1,0:T(8,128)(2,1)S(1)} %get-tuple-element.45.upper, ...), custom_call_target="tpu_custom_call" | custom-call | flops 671088640 | bytes 1000000 | tf_op jit(solution)/shard_map/inner_blocks/pallas_call | solution.py:250
  53.6 2.5 %collective-permute-done.9.even_in = f32[256,128]{1,0:T(8,128)S(1)} collective-permute-done((f32[256,128]{1,0:T(8,128)S(1)}, f32[256,128]{1,0:T(8,128)S(1)}, u32[]{:S(2)}, u32[]{:S(2)}) %collective-permute-start.9) | collective-permute-done | bytes 131104 | tf_op jit(solution)/shard_map/ppermute | solution.py:228
  56.1 0.0 collective-permute-done.10.odd_in
  56.1 1.2 %edge_blocks.9 = (f32[4,256,128]{2,1,0:T(8,128)S(1)}, f32[4,256,128]{2,1,0:T(8,128)S(1)}, f32[256,128]{1,0:T(8,128)S(1)}, f32[256,128]{1,0:T(8,128)S(1)}) custom-call(s32[2]{0:T(128)S(1)} %pad_add_fusion.info, bf16[4,256,512]{2,1,0:T(8,128)(2,1)S(1)} %get-tuple-element.44.lower, bf16[4,256,512]{2,1,0:T(8,128)(2,1)S(1)} %get-tuple-element.45.upper, ...), custom_call_target="tpu_custom_call" | custom-call | bytes 1000000 | tf_op jit(solution)/shard_map/edge_blocks/pallas_call | solution.py:262
  57.4 2.5 %collective-permute-start.11 = (f32[256,128]{1,0:T(8,128)S(1)}, f32[256,128]{1,0:T(8,128)S(1)}, u32[]{:S(2)}, u32[]{:S(2)}) collective-permute-start(f32[256,128]{1,0:T(8,128)S(1)} %get-tuple-element.79), channel_id=1, source_target_pairs={{0,1},{1,0},{2,3},{3,2},{4,5},{5,4},{6,7},{7,6},{8,9},{9,8},{10,11... | collective-permute-start | bytes 393224 | tf_op jit(solution)/shard_map/ppermute | solution.py:228
  59.9 0.0 collective-permute-start.12
  59.9 2.2 %inner_blocks.11 = (f32[4,256,128]{2,1,0:T(8,128)S(1)}, f32[4,256,128]{2,1,0:T(8,128)}) custom-call(s32[2]{0:T(128)S(1)} %pad_add_fusion.info, bf16[4,256,512]{2,1,0:T(8,128)(2,1)S(1)} %join_left.1.own, bf16[4,256,512]{2,1,0:T(8,128)(2,1)S(1)} %get-tuple-element.44.lower, bf16[4,256,512]{2,1,0:T(8,128)(2,1)S(1)} %get-tuple-element.45.upper, ...), custom_call_target="tpu_custom_call" | custom-call | flops 671088640 | bytes 1000000 | tf_op jit(solution)/shard_map/inner_blocks/pallas_call | solution.py:250
  62.1 1.7 %collective-permute-done.11.even_in = f32[256,128]{1,0:T(8,128)S(1)} collective-permute-done((f32[256,128]{1,0:T(8,128)S(1)}, f32[256,128]{1,0:T(8,128)S(1)}, u32[]{:S(2)}, u32[]{:S(2)}) %collective-permute-start.11) | collective-permute-done | bytes 131104 | tf_op jit(solution)/shard_map/ppermute | solution.py:228
  63.8 0.0 collective-permute-done.12.odd_in
  63.8 1.6 %last_residual.1 = f32[4,256,128]{2,1,0:T(8,128)} custom-call(s32[2]{0:T(128)S(1)} %pad_add_fusion.info, bf16[4,256,512]{2,1,0:T(8,128)(2,1)S(1)} %get-tuple-element.44.lower, f32[256,128]{1,0:T(8,128)S(1)} %collective-permute-done.11.even_in, f32[256,128]{1,0:T(8,128)S(1)} %collective-permute-done.12.odd_in, f32[4,256,128]{2,1,0:T(8,128)S(1)} %get-tuple-element.81.residual), custom_call_target="tpu_custom_call" | custom-call | bytes 1000000 | tf_op jit(solution)/shard_map/last_residual/pallas_call | solution.py:258
Async XLA Ops:
  1.4 2.2 %copy-start = (f32[1,1,4,512,512]{4,3,2,1,0:T(8,128)S(1)}, f32[1,1,4,512,512]{4,3,2,1,0:T(8,128)}, u32[]{:S(2)}) copy-start(f32[1,1,4,512,512]{4,3,2,1,0:T(8,128)} %operators.3) | copy-start | bytes 12582916
  3.5 1.0 %copy-start.1 = (f32[1,1,4,256,128]{4,3,2,1,0:T(8,128)S(1)}, f32[1,1,4,256,128]{4,3,2,1,0:T(8,128)}, u32[]{:S(2)}) copy-start(f32[1,1,4,256,128]{4,3,2,1,0:T(8,128)} %param.7) | copy-start | bytes 1572868
  4.6 0.7 %copy-start.2 = (s32[1,1,4,256]{3,2,1,0:T(4,128)S(1)}, s32[1,1,4,256]{3,2,1,0:T(4,128)}, u32[]{:S(2)}) copy-start(s32[1,1,4,256]{3,2,1,0:T(4,128)} %param.6) | copy-start | bytes 12292
  6.5 11.6 %collective-permute-start = (f32[256,256]{1,0:T(8,128)S(1)}, f32[256,256]{1,0:T(8,128)S(1)}, u32[]{:S(2)}, u32[]{:S(2)}) collective-permute-start(f32[256,256]{1,0:T(8,128)S(1)} %get-tuple-element.43), channel_id=1, source_target_pairs={{1,0},{2,1},{3,2},{4,3},{5,4},{6,5},{7,6},{0,7},{9,8},{10,9},{11,1... | collective-permute-start | bytes 786440 | tf_op jit(solution)/shard_map/ppermute | solution.py:239
  12.6 9.0 %collective-permute-start.1 = (f32[256,128]{1,0:T(8,128)S(1)}, f32[256,128]{1,0:T(8,128)S(1)}, u32[]{:S(2)}, u32[]{:S(2)}) collective-permute-start(f32[256,128]{1,0:T(8,128)S(1)} %get-tuple-element.46), channel_id=1, source_target_pairs={{0,1},{1,0},{2,3},{3,2},{4,5},{5,4},{6,7},{7,6},{8,9},{9,8},{10,11... | collective-permute-start | bytes 393224 | tf_op jit(solution)/shard_map/ppermute | solution.py:228
  12.6 9.0 %collective-permute-start.2 = (f32[256,128]{1,0:T(8,128)S(1)}, f32[256,128]{1,0:T(8,128)S(1)}, u32[]{:S(2)}, u32[]{:S(2)}) collective-permute-start(f32[256,128]{1,0:T(8,128)S(1)} %get-tuple-element.47), channel_id=1, source_target_pairs={{0,8},{1,2},{2,1},{3,4},{4,3},{5,6},{6,5},{7,15},{8,0},{9,10},{10,... | collective-permute-start | bytes 393224 | tf_op jit(solution)/shard_map/ppermute | solution.py:227
  22.8 8.3 %collective-permute-start.3 = (f32[256,128]{1,0:T(8,128)S(1)}, f32[256,128]{1,0:T(8,128)S(1)}, u32[]{:S(2)}, u32[]{:S(2)}) collective-permute-start(f32[256,128]{1,0:T(8,128)S(1)} %get-tuple-element.51), channel_id=1, source_target_pairs={{0,1},{1,0},{2,3},{3,2},{4,5},{5,4},{6,7},{7,6},{8,9},{9,8},{10,11... | collective-permute-start | bytes 393224 | tf_op jit(solution)/shard_map/ppermute | solution.py:228
  25.4 5.7 %collective-permute-start.4 = (f32[256,128]{1,0:T(8,128)S(1)}, f32[256,128]{1,0:T(8,128)S(1)}, u32[]{:S(2)}, u32[]{:S(2)}) collective-permute-start(f32[256,128]{1,0:T(8,128)S(1)} %get-tuple-element.52), channel_id=1, source_target_pairs={{0,8},{1,2},{2,1},{3,4},{4,3},{5,6},{6,5},{7,15},{8,0},{9,10},{10,... | collective-permute-start | bytes 393224 | tf_op jit(solution)/shard_map/ppermute | solution.py:227
  32.4 7.5 %collective-permute-start.5 = (f32[256,128]{1,0:T(8,128)S(1)}, f32[256,128]{1,0:T(8,128)S(1)}, u32[]{:S(2)}, u32[]{:S(2)}) collective-permute-start(f32[256,128]{1,0:T(8,128)S(1)} %get-tuple-element.57), channel_id=1, source_target_pairs={{0,1},{1,0},{2,3},{3,2},{4,5},{5,4},{6,7},{7,6},{8,9},{9,8},{10,11... | collective-permute-start | bytes 393224 | tf_op jit(solution)/shard_map/ppermute | solution.py:228
  35.0 4.9 %collective-permute-start.6 = (f32[256,128]{1,0:T(8,128)S(1)}, f32[256,128]{1,0:T(8,128)S(1)}, u32[]{:S(2)}, u32[]{:S(2)}) collective-permute-start(f32[256,128]{1,0:T(8,128)S(1)} %get-tuple-element.58), channel_id=1, source_target_pairs={{0,8},{1,2},{2,1},{3,4},{4,3},{5,6},{6,5},{7,15},{8,0},{9,10},{10,... | collective-permute-start | bytes 393224 | tf_op jit(solution)/shard_map/ppermute | solution.py:227
  41.1 7.3 %collective-permute-start.7 = (f32[256,128]{1,0:T(8,128)S(1)}, f32[256,128]{1,0:T(8,128)S(1)}, u32[]{:S(2)}, u32[]{:S(2)}) collective-permute-start(f32[256,128]{1,0:T(8,128)S(1)} %get-tuple-element.63), channel_id=1, source_target_pairs={{0,1},{1,0},{2,3},{3,2},{4,5},{5,4},{6,7},{7,6},{8,9},{9,8},{10,11... | collective-permute-start | bytes 393224 | tf_op jit(solution)/shard_map/ppermute | solution.py:228
  43.7 4.7 %collective-permute-start.8 = (f32[256,128]{1,0:T(8,128)S(1)}, f32[256,128]{1,0:T(8,128)S(1)}, u32[]{:S(2)}, u32[]{:S(2)}) collective-permute-start(f32[256,128]{1,0:T(8,128)S(1)} %get-tuple-element.64), channel_id=1, source_target_pairs={{0,8},{1,2},{2,1},{3,4},{4,3},{5,6},{6,5},{7,15},{8,0},{9,10},{10,... | collective-permute-start | bytes 393224 | tf_op jit(solution)/shard_map/ppermute | solution.py:227
  49.6 6.5 %collective-permute-start.9 = (f32[256,128]{1,0:T(8,128)S(1)}, f32[256,128]{1,0:T(8,128)S(1)}, u32[]{:S(2)}, u32[]{:S(2)}) collective-permute-start(f32[256,128]{1,0:T(8,128)S(1)} %get-tuple-element.69), channel_id=1, source_target_pairs={{0,1},{1,0},{2,3},{3,2},{4,5},{5,4},{6,7},{7,6},{8,9},{9,8},{10,11... | collective-permute-start | bytes 393224 | tf_op jit(solution)/shard_map/ppermute | solution.py:228
  52.2 3.9 %collective-permute-start.10 = (f32[256,128]{1,0:T(8,128)S(1)}, f32[256,128]{1,0:T(8,128)S(1)}, u32[]{:S(2)}, u32[]{:S(2)}) collective-permute-start(f32[256,128]{1,0:T(8,128)S(1)} %get-tuple-element.70), channel_id=1, source_target_pairs={{0,8},{1,2},{2,1},{3,4},{4,3},{5,6},{6,5},{7,15},{8,0},{9,10},{10,... | collective-permute-start | bytes 393224 | tf_op jit(solution)/shard_map/ppermute | solution.py:227
  57.4 6.5 %collective-permute-start.11 = (f32[256,128]{1,0:T(8,128)S(1)}, f32[256,128]{1,0:T(8,128)S(1)}, u32[]{:S(2)}, u32[]{:S(2)}) collective-permute-start(f32[256,128]{1,0:T(8,128)S(1)} %get-tuple-element.79), channel_id=1, source_target_pairs={{0,1},{1,0},{2,3},{3,2},{4,5},{5,4},{6,7},{7,6},{8,9},{9,8},{10,11... | collective-permute-start | bytes 393224 | tf_op jit(solution)/shard_map/ppermute | solution.py:228
  59.9 3.9 %collective-permute-start.12 = (f32[256,128]{1,0:T(8,128)S(1)}, f32[256,128]{1,0:T(8,128)S(1)}, u32[]{:S(2)}, u32[]{:S(2)}) collective-permute-start(f32[256,128]{1,0:T(8,128)S(1)} %get-tuple-element.80), channel_id=1, source_target_pairs={{0,8},{1,2},{2,1},{3,4},{4,3},{5,6},{6,5},{7,15},{8,0},{9,10},{10,... | collective-permute-start | bytes 393224 | tf_op jit(solution)/shard_map/ppermute | solution.py:227
where the time goes:
time: 65.7 us; the launch traced here: 65.4 us
  Pallas kernels  22.1 us (34%)
  waiting for transfers between devices  19.1 us (29%)
  starting transfers between devices  18.9 us (29%)
  local copies, waits for them, and re-layouts  3.92 us (6%)
  between operations  1.39 us (2%)
    ppermute x6, waiting for transfers between devices, exchange(): even = lax.ppermute(even, ('grp', 'sub'), evens)  16.7 us
    ppermute x6, starting transfers between devices, exchange(): even = lax.ppermute(even, ('grp', 'sub'), evens)  12.8 us
    pallas_call x6, Pallas kernels, shards(): call(functools.partial(inner_kernel, owners, step > 0), [SMEM] + [VMEM] *...  9.3 us
    pallas_call x5, Pallas kernels, shards(): call(functools.partial(edge_kernel, owners, factors), [SMEM] + [VMEM] * 6...  6.2 us
    ppermute x1, starting transfers between devices, shards(): left = lax.ppermute(left, 'sub', ring)  6.08 us
    unnamed x6, local copies, waits for them, and re-layouts  3.92 us
    pallas_call x1, Pallas kernels, shards(): call(operator_kernel, [SMEM, ANY, VMEM], [matrices] * 3, 'block_operators...  3.15 us
    ppermute x1, waiting for transfers between devices, shards(): left = lax.ppermute(left, 'sub', ring)  2.4 us
  transfers between devices with their start and end apart: 13, of which 7 were waited for; matrix products, arithmetic and copies ran while one was open for 0% of the time, Pallas kernels for 20%

commit v1 on v0

v1 whole, which is shorter than its diff:
```python
import functools

import jax
import jax.numpy as jnp
from jax import lax
from jax.experimental import pallas as pl
from jax.experimental.pallas import tpu as pltpu
from jax.sharding import PartitionSpec as P

ITERS = 6
LOWER = 1.0
UPPER = 14.0
CENTRE = (UPPER + LOWER) / 2.0
RADIUS = (UPPER - LOWER) / 2.0
BF16 = jnp.bfloat16
F32 = jnp.float32
PARTS = 2
VMEM_BYTES = 24 * 1024 * 1024


def chebyshev_factors():
    spread = CENTRE / RADIUS
    rho = 1.0 / spread
    factors = []
    for _ in range(ITERS - 1):
        rho_new = 1.0 / (2.0 * spread - rho)
        factors.append((rho_new * rho, 2.0 * rho_new / RADIUS))
        rho = rho_new
    return factors


def pairings(groups, owners):
    found = []
    for first in (0, 1):
        route = []
        for g in range(groups):
            for s in range(owners):
                t = s + 1 if (s - first) % 2 == 0 else s - 1
                h = g
                if t < 0 or t >= owners:
                    t = s
                    h = g ^ 1
                if h < groups:
                    route.append((g * owners + s, h * owners + t))
        found.append(route)
    return found


def halves(x):
    high = x.astype(BF16)
    return high, (x - high.astype(F32)).astype(BF16)


def operand(x):
    high, low = halves(x)
    return jnp.concatenate([high, low], axis=0), high


def split_dot(cases, matrix):
    both, high = cases
    h = matrix.shape[0] // 2
    tall = jnp.dot(both, matrix[:h], preferred_element_type=F32)
    rows = high.shape[0]
    return tall[:rows] + tall[rows:] + jnp.dot(high, matrix[h:], preferred_element_type=F32)


def dot_nt(a, b):
    return lax.dot_general(a, b, (((1,), (1,)), ((), ())), preferred_element_type=F32)


def signed_placement(pairs):
    h = pairs.shape[1]
    rows = lax.broadcasted_iota(jnp.int32, (h, h), 0)
    picked = jnp.abs(pairs) - 1
    sign = jnp.where(pairs > 0, 1.0, -1.0)
    return jnp.where(rows == picked, sign, 0.0).astype(BF16)


def exists_of(count, pos, owners, slot):
    there = jnp.logical_and(slot < count, jnp.logical_or(pos < owners - 1, slot != count - 1))
    return jnp.where(there, 1.0, 0.0)


def row(marks, k):
    return marks[k, pl.ds(0, 1), :]


def first_kernel(owners, operators, counts, pairs, gap, upper_left, lower_left, residual, direction, ahead_out, even_out, odd_out, marks, pairs_at, top, source, sems):
    slots, h = residual.shape[0], residual.shape[2]
    copies = [
        pltpu.make_async_copy(pairs.at[0, 0], pairs_at, sems.at[0]),
        pltpu.make_async_copy(operators.at[0, 0, 0, pl.ds(0, h)], top, sems.at[1]),
        pltpu.make_async_copy(gap.at[0, 0], source, sems.at[2]),
    ]
    for copy in copies:
        copy.start()
    pos = lax.axis_index("sub")
    count = counts[0, 0]
    is_even = lax.rem(pos, 2) == 0
    shape = marks.shape[1:]
    for j in range(slots):
        here = exists_of(count, pos, owners, j)
        marks[j] = jnp.full(shape, jnp.where(count - 1 == j, here, 0.0), F32)
        marks[slots + 1 + j] = jnp.full(shape, jnp.where(pos == 0, 0.0, here) if j == 0 else here, F32)
    marks[slots] = jnp.full(shape, jnp.where(is_even, 1.0, 0.0), F32)
    copies[0].wait()
    place = signed_placement(pairs_at[pl.ds(0, 1), :])
    copies[1].wait()
    placed = [jnp.dot(place, part, preferred_element_type=F32).astype(BF16) for part in halves(top[...])]
    square = [dot_nt(place, part[:, :h]) for part in placed]
    square = square[0] + square[1]
    upper_left[...] = square[: h // 2]
    lower_left[...] = square[h // 2 :]
    copies[2].wait()
    for j in range(slots):
        residual[j] = source[j].T * exists_of(count, pos, owners, j)
        direction[j] = residual[j] / CENTRE
    both, high = operand(direction[0])
    tall = dot_nt(both, placed[0][:, h:])
    rows = high.shape[0]
    behind = -(tall[:rows] + tall[rows:] + dot_nt(high, placed[1][:, h:]))
    ahead = direction[count - 1]
    ahead_out[...] = ahead
    even_out[...] = jnp.where(is_even, ahead, behind)
    odd_out[...] = jnp.where(is_even, behind, ahead)


def operator_kernel(operators, pairs, marks, own_out, lower_out, upper_out, whole, sems):
    slots, h = pairs.shape
    copies = [pltpu.make_async_copy(operators.at[0, 0, j], whole.at[j], sems.at[j]) for j in range(slots)]
    for copy in copies:
        copy.start()
    unit = signed_placement(lax.broadcasted_iota(jnp.int32, (1, h), 1) + 1)
    for j in range(slots):
        copies[j].wait()
        place = signed_placement(pairs[pl.ds(j, 1), :])
        taken = marks[slots + 1 + j, pl.ds(0, 1), pl.ds(0, 1)]
        squares, diagonal = [], []
        for k, part in enumerate(halves(whole[j])):
            rows = pl.ds(k * h, h)
            placed = jnp.dot(place, part[:h], preferred_element_type=F32).astype(BF16)
            upper_out[j, rows, :] = -dot_nt(unit, placed[:, h:]).astype(BF16)
            lower_out[j, rows, :] = (dot_nt(place, part[h:, :h]) * -taken).astype(BF16)
            squares.append(dot_nt(place, placed[:, :h]))
            diagonal.append(dot_nt(unit, part[h:, h:]))
        if j > 0:
            before = marks[j - 1, pl.ds(0, 1), pl.ds(0, 1)]
            put_halves(own_out, j - 1, previous + jnp.where(before > 0.5, 0.0, squares[0] + squares[1]))
        previous = diagonal[0] + diagonal[1]
    put_halves(own_out, slots - 1, previous)


def put_halves(out, j, matrix):
    h = matrix.shape[0]
    out[j, pl.ds(0, h), :], out[j, pl.ds(h, h), :] = halves(matrix)


def inner_step(own, lower, upper, marks, direction, residual, factors, residual_out, first_part, last_part):
    slots = len(direction)
    cases = [operand(block) for block in direction]
    last, last_residual = 0.0, 0.0
    for j in range(slots):
        image = split_dot(cases[j], own[j])
        if j > 0:
            image += split_dot(cases[j - 1], lower[j])
        if j + 1 < slots:
            image += split_dot(cases[j + 1], upper[j + 1])
        rest = residual[j] - image
        if factors is None:
            residual_out[j] = rest.T
            continue
        residual_out[j] = rest
        if j == 0:
            first_part[...] = factors[0] * direction[0] + factors[1] * rest
        last += row(marks, j) * direction[j]
        last_residual += row(marks, j) * rest
    if factors is not None:
        last_part[...] = factors[0] * last + factors[1] * last_residual


def first_inner_kernel(factors, own, lower, upper, marks, direction, residual, residual_out, first_part, last_part):
    slots = direction.shape[0]
    blocks, rests = [direction[j] for j in range(slots)], [residual[j] for j in range(slots)]
    inner_step(own, lower, upper, marks, blocks, rests, factors, residual_out, first_part, last_part)


def inner_kernel(before, factors, joins, parts, own, lower, upper, marks, direction, residual, total, *rest):
    rest = list(rest)
    slots, h = direction.shape[0], direction.shape[2]
    across = jnp.concatenate([part[...] for part in rest[:parts]], axis=0)
    behind = jnp.concatenate([part[...] for part in rest[parts : 2 * parts]], axis=0)
    rest = rest[2 * parts :]
    if joins:
        left = jnp.concatenate([rest[0][...], rest[1][...]], axis=0)
        joined = rest[-1]
        rest = rest[2:-1]
        for j in range(slots):
            matrix = own[j, pl.ds(0, h), :].astype(F32) + own[j, pl.ds(h, h), :].astype(F32)
            put_halves(joined, j, matrix + left * marks[j, pl.ds(0, 1), pl.ds(0, 1)])
        own = joined
    residual_out, total_out = rest[:2]
    direction_out, first_part, last_part = rest[2:] if factors is not None else (None, None, None)
    blocks, rests = [], []
    for j in range(slots):
        left_over = residual[j] - row(marks, j) * behind
        if j == 0:
            left_over -= across
        block = before[0] * direction[j] + before[1] * left_over
        if direction_out is not None:
            direction_out[j] = block
            total_out[j] = total[j] + block
        else:
            total_out[j] = (total[j] + block).T
        blocks.append(block)
        rests.append(left_over)
    inner_step(own, lower, upper, marks, blocks, rests, factors, residual_out, first_part, last_part)


def received(marks, even, odd, slots):
    is_even = row(marks, slots) > 0.5
    return jnp.where(is_even, odd, even), jnp.where(is_even, even, odd)


def edge_kernel(factors, joins, start, outs, lower, upper, marks, even_in, odd_in, first_part, last_part, *rest):
    slots = lower.shape[0]
    if joins:
        upper_left, lower_left, ahead, *rest = rest
    across_out, behind_out, *sent_out = rest
    rows = pl.ds(start, even_in.shape[0])
    before, behind = received(marks, even_in[...], odd_in[...], slots)
    across = split_dot(operand(before), lower[0])
    if joins:
        left = jnp.concatenate([upper_left[...], lower_left[...]], axis=0)
        behind += split_dot(operand(ahead[...]), jnp.concatenate(halves(left), axis=0))
    across_out[...] = across
    behind_out[...] = behind
    exists = sum(row(marks, j) for j in range(slots))
    alone = row(marks, 0)
    first = first_part[rows, :] - factors[1] * (across + alone * behind)
    last = last_part[rows, :] - factors[1] * (exists * behind + alone * across)
    sent = split_dot(operand(first), upper[0])
    is_even = row(marks, slots) > 0.5
    even, odd = jnp.where(is_even, last, sent), jnp.where(is_even, sent, last)
    height = even.shape[0] // outs
    for k in range(outs):
        sent_out[2 * k][...] = even[k * height : (k + 1) * height]
        sent_out[2 * k + 1][...] = odd[k * height : (k + 1) * height]


def last_kernel(parts, lower, marks, *rest):
    slots = lower.shape[0]
    even = jnp.concatenate([part[...] for part in rest[:parts]], axis=0)
    odd = jnp.concatenate([part[...] for part in rest[parts : 2 * parts]], axis=0)
    residual, out, ready, sems = rest[2 * parts :]
    before, behind = received(marks, even, odd, slots)
    behind = behind.T
    copies = [pltpu.make_async_copy(ready.at[j], out.at[0, 0, j], sems.at[j]) for j in range(slots)]
    for j in range(1, slots):
        ready[j] = residual[j] - marks[j, pl.ds(0, 1), pl.ds(0, behind.shape[1])] * behind
        copies[j].start()
    across = split_dot(operand(before), lower[0])
    ready[0] = residual[0] - marks[0, pl.ds(0, 1), pl.ds(0, behind.shape[1])] * behind - across.T
    copies[0].start()
    for copy in copies:
        copy.wait()


VMEM = pl.BlockSpec(memory_space=pltpu.VMEM)
SMEM = pl.BlockSpec(memory_space=pltpu.SMEM)
HBM = pl.BlockSpec(memory_space=pltpu.HBM)


def in_hbm(x):
    return pltpu.with_memory_space_constraint(x, pltpu.HBM)


def call(kernel, name, ins, outs, scratch=(), out_space=VMEM):
    return pl.pallas_call(
        kernel,
        in_specs=ins,
        out_specs=[out_space] * len(outs),
        out_shape=[jax.ShapeDtypeStruct(shape, kind) for shape, kind in outs],
        scratch_shapes=list(scratch),
        compiler_params=pltpu.CompilerParams(vmem_limit_bytes=VMEM_BYTES),
        name=name,
    )


def shards(groups, owners, operators, counts, pair_rows, gap):
    slots, h, cases = gap.shape[2:]
    m = operators.shape[-1]
    width = cases // PARTS
    evens, odds = pairings(groups, owners)
    ring = [((s + 1) % owners, s) for s in range(owners)]
    field = ((slots, cases, h), F32)
    turned = ((slots, h, cases), F32)
    block = ((cases, h), F32)
    part = ((width, h), F32)
    matrices = ((slots, 2 * h, h), BF16)

    def exchange(even, odd):
        odd = lax.ppermute(odd, ("grp", "sub"), odds)
        even = lax.ppermute(even, ("grp", "sub"), evens)
        return even, odd

    operators = in_hbm(operators)
    *lefts, residual, direction, ahead, even, odd, marks = call(
        functools.partial(first_kernel, owners),
        "first_messages",
        [HBM, SMEM, HBM, HBM],
        [((h // 2, h), F32)] * 2 + [field, field, block, block, block, ((2 * slots + 1, 8, h), F32)],
        [
            pltpu.VMEM((slots, h), jnp.int32),
            pltpu.VMEM((h, m), F32),
            pltpu.VMEM(*turned),
            pltpu.SemaphoreType.DMA((3,)),
        ],
    )(operators, counts, in_hbm(pair_rows), in_hbm(gap))
    sent = [exchange(even, odd)]
    lefts = [lax.ppermute(half, "sub", ring) for half in lefts]
    own, lower, upper = call(
        operator_kernel,
        "block_operators",
        [HBM, VMEM, VMEM],
        [matrices] * 3,
        [pltpu.VMEM((slots, m, m), F32), pltpu.SemaphoreType.DMA((slots,))],
    )(operators, pair_rows[0, 0], marks)
    factors = chebyshev_factors() + [None]
    residual, first, last = call(
        functools.partial(first_inner_kernel, factors[0]), "first_inner_blocks", [VMEM] * 6, [field, block, block]
    )(own, lower, upper, marks, direction, residual)
    total = direction
    for step in range(1, ITERS):
        joins = step == 1
        extra = [*lefts, ahead] if joins else []
        across, behind, sending = [], [], []
        for k, (even, odd) in enumerate(sent):
            outs = PARTS if joins else 1
            got = call(
                functools.partial(edge_kernel, factors[step - 1], joins, k * width, outs),
                "edge_blocks",
                [VMEM] * (7 + len(extra)),
                [block if joins else part] * 2 + [part] * (2 * outs),
            )(lower, upper, marks, even, odd, first, last, *extra)
            across.append(got[0])
            behind.append(got[1])
            sending += [exchange(got[2 + 2 * n], got[3 + 2 * n]) for n in range(outs)]
        sent = sending
        extra = lefts if joins else []
        ends = step == ITERS - 1
        outs = ([turned] * 2 if ends else [field] * 3 + [block] * 2) + ([matrices] if joins else [])
        got = call(
            functools.partial(inner_kernel, factors[step - 1], factors[step], joins, len(across)),
            "inner_blocks",
            [VMEM] * (7 + 2 * len(across) + len(extra)),
            outs,
        )(own, lower, upper, marks, direction, residual, total, *across, *behind, *extra)
        residual, total = got[:2]
        if not ends:
            direction, first, last = got[2:5]
        if joins:
            own = got[5]
    (residual,) = call(
        functools.partial(last_kernel, PARTS),
        "last_residual",
        [VMEM] * (3 + 2 * PARTS),
        [(gap.shape, F32)],
        [pltpu.VMEM(*turned), pltpu.SemaphoreType.DMA((slots,))],
        HBM,
    )(lower, marks, *(even for even, _ in sent), *(odd for _, odd in sent), residual)
    return total[None, None], residual


def solution(mesh):
    groups, owners = mesh.shape["grp"], mesh.shape["sub"]
    return jax.shard_map(
        functools.partial(shards, groups, owners),
        mesh=mesh,
        in_specs=(
            P("grp", "sub", None, None, None),
            P("grp", "sub"),
            P("grp", "sub", None, None),
            P("grp", "sub", None, None, None),
        ),
        out_specs=(P("grp", "sub", None, None, None), P("grp", "sub", None, None, None)),
        check_vma=False,
    )
```

time: 65.7 us -> 56.8 us (0.86)
  starting transfers between devices: 18.9 us -> 36 us
  waiting for transfers between devices: 19.1 us -> 2.43 us
  Pallas kernels: 22.1 us -> 16.3 us
  local copies, waits for them, and re-layouts: 3.92 us -> 0.01 us
    ppermute x6 -> x11, starting transfers between devices: 12.8 us -> 30.5 us  [exchange(): even = lax.ppermute(even, ('grp', 'sub'), evens)]
    ppermute x6 -> x11, waiting for transfers between devices: 16.7 us -> 2.39 us  [exchange(): even = lax.ppermute(even, ('grp', 'sub'), evens)]
    pallas_call x15 -> x18, Pallas kernels: 22.1 us -> 16.3 us  [the longest x5 4.89 us: shards(): call(functools.partial(inner_kernel, factors[step - 1], factors[step], jo...]
    unnamed x6 -> x2, local copies, waits for them, and re-layouts: 3.92 us -> 0.01 us
    ppermute x1 -> x2, waiting for transfers between devices: 2.4 us -> 0.01 us  [shards(): lefts = [lax.ppermute(half, 'sub', ring) for half in lefts]]
    ppermute x1 -> x2, starting transfers between devices: 6.08 us -> 5.45 us  [shards(): lefts = [lax.ppermute(half, 'sub', ring) for half in lefts]]
  transfers between devices with their start and end apart: 13 -> 24, of which waited for: 7 -> 2; matrix products, arithmetic and copies ran while one was open for 0% -> 0% of each run, Pallas kernels for 20% -> 23%
where the time goes in v1:
time: 56.8 us; the launch traced here: 56.3 us
  starting transfers between devices  36 us (63%)
  Pallas kernels  16.3 us (29%)
  waiting for transfers between devices  2.43 us (4%)
  between operations  1.51 us (3%)
    ppermute x11, starting transfers between devices, exchange(): even = lax.ppermute(even, ('grp', 'sub'), evens)  30.5 us
    ppermute x2, starting transfers between devices, shards(): lefts = [lax.ppermute(half, 'sub', ring) for half in lefts]  5.45 us
    pallas_call x5, Pallas kernels, shards(): call(functools.partial(inner_kernel, factors[step - 1], factors[step], jo...  4.89 us
    pallas_call x1, Pallas kernels, shards(): call(operator_kernel, 'block_operators', [HBM, VMEM, VMEM], [matrices] *...  4.38 us
    pallas_call x9, Pallas kernels, shards(): call(functools.partial(edge_kernel, factors[step - 1], joins, k * width,...  3.39 us
    ppermute x11, waiting for transfers between devices, exchange(): even = lax.ppermute(even, ('grp', 'sub'), evens)  2.39 us
    pallas_call x1, Pallas kernels, shards(): call(functools.partial(first_kernel, owners), 'first_messages', [HBM, SME...  1.93 us
  transfers between devices with their start and end apart: 24, of which 2 were waited for; matrix products, arithmetic and copies ran while one was open for 0% of the time, Pallas kernels for 23%

profile of v1, /device:TPU:0, one launch (start us, length us, event | category | flops | bytes accessed | tf_op | source)
XLA Modules:
  0.0 56.3 jit_solution(5701836407786880658)
XLA Ops:
  1.3 1.9 %first_messages.1 = (f32[128,256]{1,0:T(8,128)S(1)}, f32[128,256]{1,0:T(8,128)S(1)}, f32[4,128,256]{2,1,0:T(8,128)S(1)}, f32[4,128,256]{2,1,0:T(8,128)S(1)}, f32...) custom-call(f32[1,1,4,512,512]{4,3,2,1,0:T(8,128)} %operators.3, ...), custom_call_target="tpu_custom_call" | custom-call | tf_op jit(solution)/shard_map/first_messages/pallas_call | solution.py:307
  3.2 3.0 %collective-permute-start = (f32[128,256]{1,0:T(8,128)S(1)}, f32[128,256]{1,0:T(8,128)S(1)}, u32[]{:S(2)}, u32[]{:S(2)}) collective-permute-start(f32[128,256]{1,0:T(8,128)S(1)} %get-tuple-element.84), channel_id=1, source_target_pairs={{0,1},{1,0},{2,3},{3,2},{4,5},{5,4},{6,7},{7,6},{8,9},{9,8},{10,11... | collective-permute-start | bytes 393224 | tf_op jit(solution)/shard_map/ppermute | solution.py:303
  6.3 0.0 collective-permute-start.1
  6.3 3.5 %collective-permute-start.2 = (f32[128,256]{1,0:T(8,128)S(1)}, f32[128,256]{1,0:T(8,128)S(1)}, u32[]{:S(2)}, u32[]{:S(2)}) collective-permute-start(f32[128,256]{1,0:T(8,128)S(1)} %get-tuple-element.88), channel_id=1, source_target_pairs={{1,0},{2,1},{3,2},{4,3},{5,4},{6,5},{7,6},{0,7},{9,8},{10,9},{11,1... | collective-permute-start | bytes 393224 | tf_op jit(solution)/shard_map/ppermute | solution.py:320
  9.8 1.9 %collective-permute-start.3 = (f32[128,256]{1,0:T(8,128)S(1)}, f32[128,256]{1,0:T(8,128)S(1)}, u32[]{:S(2)}, u32[]{:S(2)}) collective-permute-start(f32[128,256]{1,0:T(8,128)S(1)} %get-tuple-element.89), channel_id=1, source_target_pairs={{1,0},{2,1},{3,2},{4,3},{5,4},{6,5},{7,6},{0,7},{9,8},{10,9},{11,1... | collective-permute-start | bytes 393224 | tf_op jit(solution)/shard_map/ppermute | solution.py:320
  11.7 4.4 %block_operators.1 = (bf16[4,512,256]{2,1,0:T(8,128)(2,1)S(1)}, bf16[4,512,256]{2,1,0:T(8,128)(2,1)S(1)}, bf16[4,512,256]{2,1,0:T(8,128)(2,1)S(1)}) custom-call(f32[1,1,4,512,512]{4,3,2,1,0:T(8,128)} %operators.3, s32[4,256]{1,0:T(4,128)S(1)} %bitcast.2, f32[9,8,256]{2,1,0:T(8,128)S(1)} %get-tuple-element.77.marks), custom_call_target="tpu_custom_call" | custom-call | tf_op jit(solution)/shard_map/block_operators/pallas_call | solution.py:321
  16.1 0.7 %first_inner_blocks.1 = (f32[4,128,256]{2,1,0:T(8,128)S(1)}, f32[128,256]{1,0:T(8,128)S(1)}, f32[128,256]{1,0:T(8,128)S(1)}) custom-call(bf16[4,512,256]{2,1,0:T(8,128)(2,1)S(1)} %get-tuple-element.78.own, bf16[4,512,256]{2,1,0:T(8,128)(2,1)S(1)} %get-tuple-element.79.lower, bf16[4,512,256]{2,1,0:T(8,128)(2,1)S(1)} %get-tuple-element.80.upper, ...), custom_call_target="tpu_custom_call" | custom-call | tf_op jit(solution)/shard_map/first_inner_blocks/pallas_call | solution.py:329
  16.8 0.6 %collective-permute-done.even_in = f32[128,256]{1,0:T(8,128)S(1)} collective-permute-done((f32[128,256]{1,0:T(8,128)S(1)}, f32[128,256]{1,0:T(8,128)S(1)}, u32[]{:S(2)}, u32[]{:S(2)}) %collective-permute-start) | collective-permute-done | bytes 131104 | tf_op jit(solution)/shard_map/ppermute | solution.py:303
  17.4 0.0 collective-permute-done.1.odd_in
  17.4 0.0 collective-permute-done.2.rest_0_.rest_2_
  17.5 0.0 collective-permute-done.3.rest_1_.rest_3_
  17.5 0.5 edge_blocks.9
  18.0 2.5 %collective-permute-start.4 = (f32[64,256]{1,0:T(8,128)S(1)}, f32[64,256]{1,0:T(8,128)S(1)}, u32[]{:S(2)}, u32[]{:S(2)}) collective-permute-start(f32[64,256]{1,0:T(8,128)S(1)} %get-tuple-element.97), channel_id=1, source_target_pairs={{0,1},{1,0},{2,3},{3,2},{4,5},{5,4},{6,7},{7,6},{8,9},{9,8},{10,11... | collective-permute-start | bytes 196616 | tf_op jit(solution)/shard_map/ppermute | solution.py:303
  20.5 0.0 collective-permute-start.5
  20.5 3.0 %collective-permute-start.6 = (f32[64,256]{1,0:T(8,128)S(1)}, f32[64,256]{1,0:T(8,128)S(1)}, u32[]{:S(2)}, u32[]{:S(2)}) collective-permute-start(f32[64,256]{1,0:T(8,128)S(1)} %get-tuple-element.102), channel_id=1, source_target_pairs={{0,1},{1,0},{2,3},{3,2},{4,5},{5,4},{6,7},{7,6},{8,9},{9,8},{10,11... | collective-permute-start | bytes 196616 | tf_op jit(solution)/shard_map/ppermute | solution.py:303
  23.6 0.0 collective-permute-start.7
  23.6 1.0 %inner_blocks.5 = (f32[4,128,256]{2,1,0:T(8,128)S(1)}, f32[4,128,256]{2,1,0:T(8,128)S(1)}, f32[4,128,256]{2,1,0:T(8,128)S(1)}, f32[128,256]{1,0:T(8,128)S(1)}, f...) custom-call(bf16[4,512,256]{2,1,0:T(8,128)(2,1)S(1)} %get-tuple-element.78.own, ...), custom_call_target="tpu_custom_call" | custom-call | tf_op jit(solution)/shard_map/inner_blocks/pallas_call | solution.py:352
  24.6 0.0 collective-permute-done.4.even_in
  24.6 0.0 collective-permute-done.5.odd_in
  24.6 0.4 edge_blocks.10
  25.0 3.1 %collective-permute-start.8 = (f32[64,256]{1,0:T(8,128)S(1)}, f32[64,256]{1,0:T(8,128)S(1)}, u32[]{:S(2)}, u32[]{:S(2)}) collective-permute-start(f32[64,256]{1,0:T(8,128)S(1)} %get-tuple-element.110), channel_id=1, source_target_pairs={{0,1},{1,0},{2,3},{3,2},{4,5},{5,4},{6,7},{7,6},{8,9},{9,8},{10,11... | collective-permute-start | bytes 196616 | tf_op jit(solution)/shard_map/ppermute | solution.py:303
  28.1 0.0 collective-permute-start.9
  28.1 0.0 collective-permute-done.6.even_in
  28.1 0.0 collective-permute-done.7.odd_in
  28.1 0.4 edge_blocks.11
  28.5 2.7 %collective-permute-start.10 = (f32[64,256]{1,0:T(8,128)S(1)}, f32[64,256]{1,0:T(8,128)S(1)}, u32[]{:S(2)}, u32[]{:S(2)}) collective-permute-start(f32[64,256]{1,0:T(8,128)S(1)} %get-tuple-element.115), channel_id=1, source_target_pairs={{0,1},{1,0},{2,3},{3,2},{4,5},{5,4},{6,7},{7,6},{8,9},{9,8},{10,11... | collective-permute-start | bytes 196616 | tf_op jit(solution)/shard_map/ppermute | solution.py:303
  31.1 0.0 collective-permute-start.11
  31.1 0.8 %inner_blocks.6 = (f32[4,128,256]{2,1,0:T(8,128)S(1)}, f32[4,128,256]{2,1,0:T(8,128)S(1)}, f32[4,128,256]{2,1,0:T(8,128)S(1)}, f32[128,256]{1,0:T(8,128)S(1)}, f32[128,256]{1,0:T(8,128)S(1)}) custom-call(bf16[4,512,256]{2,1,0:T(8,128)(2,1)S(1)} %get-tuple-element.93.own, bf16[4,512,256]{2,1,0:T(8,128)(2,1)S(1)} %get-tuple-element.79.lower, ...), custom_call_target="tpu_custom_call" | custom-call | tf_op jit(solution)/shard_map/inner_blocks/pallas_call | solution.py:352
  31.9 0.0 collective-permute-done.8.even_in
  32.0 0.0 collective-permute-done.9.odd_in
  32.0 0.4 edge_blocks.12
  32.3 3.0 %collective-permute-start.12 = (f32[64,256]{1,0:T(8,128)S(1)}, f32[64,256]{1,0:T(8,128)S(1)}, u32[]{:S(2)}, u32[]{:S(2)}) collective-permute-start(f32[64,256]{1,0:T(8,128)S(1)} %get-tuple-element.123), channel_id=1, source_target_pairs={{0,1},{1,0},{2,3},{3,2},{4,5},{5,4},{6,7},{7,6},{8,9},{9,8},{10,11... | collective-permute-start | bytes 196616 | tf_op jit(solution)/shard_map/ppermute | solution.py:303
  35.3 0.0 collective-permute-start.13
  35.3 0.0 collective-permute-done.10.even_in
  35.3 0.0 collective-permute-done.11.odd_in
  35.3 0.4 edge_blocks.13
  35.7 2.2 %collective-permute-start.14 = (f32[64,256]{1,0:T(8,128)S(1)}, f32[64,256]{1,0:T(8,128)S(1)}, u32[]{:S(2)}, u32[]{:S(2)}) collective-permute-start(f32[64,256]{1,0:T(8,128)S(1)} %get-tuple-element.128), channel_id=1, source_target_pairs={{0,1},{1,0},{2,3},{3,2},{4,5},{5,4},{6,7},{7,6},{8,9},{9,8},{10,11... | collective-permute-start | bytes 196616 | tf_op jit(solution)/shard_map/ppermute | solution.py:303
  37.9 0.0 collective-permute-start.15
  37.9 0.8 %inner_blocks.7 = (f32[4,128,256]{2,1,0:T(8,128)S(1)}, f32[4,128,256]{2,1,0:T(8,128)S(1)}, f32[4,128,256]{2,1,0:T(8,128)S(1)}, f32[128,256]{1,0:T(8,128)S(1)}, f32[128,256]{1,0:T(8,128)S(1)}) custom-call(bf16[4,512,256]{2,1,0:T(8,128)(2,1)S(1)} %get-tuple-element.93.own, bf16[4,512,256]{2,1,0:T(8,128)(2,1)S(1)} %get-tuple-element.79.lower, ...), custom_call_target="tpu_custom_call" | custom-call | tf_op jit(solution)/shard_map/inner_blocks/pallas_call | solution.py:352
  38.7 0.0 collective-permute-done.12.even_in
  38.8 0.0 collective-permute-done.13.odd_in
  38.8 0.4 edge_blocks.14
  39.1 2.8 %collective-permute-start.16 = (f32[64,256]{1,0:T(8,128)S(1)}, f32[64,256]{1,0:T(8,128)S(1)}, u32[]{:S(2)}, u32[]{:S(2)}) collective-permute-start(f32[64,256]{1,0:T(8,128)S(1)} %get-tuple-element.136), channel_id=1, source_target_pairs={{0,1},{1,0},{2,3},{3,2},{4,5},{5,4},{6,7},{7,6},{8,9},{9,8},{10,11... | collective-permute-start | bytes 196616 | tf_op jit(solution)/shard_map/ppermute | solution.py:303
  41.9 0.0 collective-permute-start.17
  41.9 0.0 collective-permute-done.14.even_in
  41.9 0.0 collective-permute-done.15.odd_in
  41.9 0.4 edge_blocks.15
  42.3 3.0 %collective-permute-start.18 = (f32[64,256]{1,0:T(8,128)S(1)}, f32[64,256]{1,0:T(8,128)S(1)}, u32[]{:S(2)}, u32[]{:S(2)}) collective-permute-start(f32[64,256]{1,0:T(8,128)S(1)} %get-tuple-element.141), channel_id=1, source_target_pairs={{0,1},{1,0},{2,3},{3,2},{4,5},{5,4},{6,7},{7,6},{8,9},{9,8},{10,11... | collective-permute-start | bytes 196616 | tf_op jit(solution)/shard_map/ppermute | solution.py:303
  45.3 0.0 collective-permute-start.19
  45.3 0.8 %inner_blocks.8 = (f32[4,128,256]{2,1,0:T(8,128)S(1)}, f32[4,128,256]{2,1,0:T(8,128)S(1)}, f32[4,128,256]{2,1,0:T(8,128)S(1)}, f32[128,256]{1,0:T(8,128)S(1)}, f32[128,256]{1,0:T(8,128)S(1)}) custom-call(bf16[4,512,256]{2,1,0:T(8,128)(2,1)S(1)} %get-tuple-element.93.own, bf16[4,512,256]{2,1,0:T(8,128)(2,1)S(1)} %get-tuple-element.79.lower, ...), custom_call_target="tpu_custom_call" | custom-call | tf_op jit(solution)/shard_map/inner_blocks/pallas_call | solution.py:352
  46.1 0.0 collective-permute-done.16.even_in
  46.1 0.0 collective-permute-done.17.odd_in
  46.1 0.4 edge_blocks.16
  46.5 3.1 %collective-permute-start.20 = (f32[64,256]{1,0:T(8,128)S(1)}, f32[64,256]{1,0:T(8,128)S(1)}, u32[]{:S(2)}, u32[]{:S(2)}) collective-permute-start(f32[64,256]{1,0:T(8,128)S(1)} %get-tuple-element.147), channel_id=1, source_target_pairs={{0,1},{1,0},{2,3},{3,2},{4,5},{5,4},{6,7},{7,6},{8,9},{9,8},{10,11... | collective-permute-start | bytes 196616 | tf_op jit(solution)/shard_map/ppermute | solution.py:303
  49.6 0.0 collective-permute-start.22
  49.6 0.0 collective-permute-done.18.even_in
  49.6 0.4 edge_blocks.17
  50.0 2.0 %collective-permute-start.21 = (f32[64,256]{1,0:T(8,128)S(1)}, f32[64,256]{1,0:T(8,128)S(1)}, u32[]{:S(2)}, u32[]{:S(2)}) collective-permute-start(f32[64,256]{1,0:T(8,128)S(1)} %get-tuple-element.148), channel_id=1, source_target_pairs={{0,1},{1,0},{2,3},{3,2},{4,5},{5,4},{6,7},{7,6},{8,9},{9,8},{10,11... | collective-permute-start | bytes 196616 | tf_op jit(solution)/shard_map/ppermute | solution.py:303
  52.0 1.5 %inner_blocks.9 = (f32[4,256,128]{2,1,0:T(8,128)S(1)}, f32[4,256,128]{2,1,0:T(8,128)}) custom-call(bf16[4,512,256]{2,1,0:T(8,128)(2,1)S(1)} %get-tuple-element.93.own, bf16[4,512,256]{2,1,0:T(8,128)(2,1)S(1)} %get-tuple-element.79.lower, bf16[4,512,256]{2,1,0:T(8,128)(2,1)S(1)} %get-tuple-element.80.upper, f32[9,8,256]{2,1,0:T(8,128)S(1)} %get-tuple-element.77.marks, ...), custom_call_target="tpu_custom_call" | custom-call | tf_op jit(solution)/shard_map/inner_blocks/pallas_call | solution.py:352
  53.5 0.0 collective-permute-done.20.rest_0_
  53.5 0.0 collective-permute-done.22.rest_2_
  53.5 1.8 %collective-permute-done.21.rest_1_ = f32[64,256]{1,0:T(8,128)S(1)} collective-permute-done((f32[64,256]{1,0:T(8,128)S(1)}, f32[64,256]{1,0:T(8,128)S(1)}, u32[]{:S(2)}, u32[]{:S(2)}) %collective-permute-start.21) | collective-permute-done | bytes 65568 | tf_op jit(solution)/shard_map/ppermute | solution.py:303
  55.3 0.0 collective-permute-done.23.rest_3_
  55.3 1.0 %last_residual.1 = f32[1,1,4,256,128]{4,3,2,1,0:T(8,128)} custom-call(bf16[4,512,256]{2,1,0:T(8,128)(2,1)S(1)} %get-tuple-element.79.lower, f32[9,8,256]{2,1,0:T(8,128)S(1)} %get-tuple-element.77.marks, f32[64,256]{1,0:T(8,128)S(1)} %collective-permute-done.20.rest_0_, f32[64,256]{1,0:T(8,128)S(1)} %collective-permute-done.21.rest_1_, ...), custom_call_target="tpu_custom_call" | custom-call | tf_op jit(solution)/shard_map/last_residual/pallas_call | solution.py:363
  (4 shorter events, 0.0 us)
Async XLA Ops:
  0.6 11.1 %copy-start = (s32[1,1,4,256]{3,2,1,0:T(4,128)S(1)}, s32[1,1,4,256]{3,2,1,0:T(4,128)}, u32[]{:S(2)}) copy-start(s32[1,1,4,256]{3,2,1,0:T(4,128)} %pairs.1) | copy-start | bytes 12292
  3.2 14.2 %collective-permute-start = (f32[128,256]{1,0:T(8,128)S(1)}, f32[128,256]{1,0:T(8,128)S(1)}, u32[]{:S(2)}, u32[]{:S(2)}) collective-permute-start(f32[128,256]{1,0:T(8,128)S(1)} %get-tuple-element.84), channel_id=1, source_target_pairs={{0,1},{1,0},{2,3},{3,2},{4,5},{5,4},{6,7},{7,6},{8,9},{9,8},{10,11... | collective-permute-start | bytes 393224 | tf_op jit(solution)/shard_map/ppermute | solution.py:303
  6.3 11.2 %collective-permute-start.1 = (f32[128,256]{1,0:T(8,128)S(1)}, f32[128,256]{1,0:T(8,128)S(1)}, u32[]{:S(2)}, u32[]{:S(2)}) collective-permute-start(f32[128,256]{1,0:T(8,128)S(1)} %get-tuple-element.85), channel_id=1, source_target_pairs={{0,8},{1,2},{2,1},{3,4},{4,3},{5,6},{6,5},{7,15},{8,0},{9,10},{10,... | collective-permute-start | bytes 393224 | tf_op jit(solution)/shard_map/ppermute | solution.py:302
  6.3 11.2 %collective-permute-start.2 = (f32[128,256]{1,0:T(8,128)S(1)}, f32[128,256]{1,0:T(8,128)S(1)}, u32[]{:S(2)}, u32[]{:S(2)}) collective-permute-start(f32[128,256]{1,0:T(8,128)S(1)} %get-tuple-element.88), channel_id=1, source_target_pairs={{1,0},{2,1},{3,2},{4,3},{5,4},{6,5},{7,6},{0,7},{9,8},{10,9},{11,1... | collective-permute-start | bytes 393224 | tf_op jit(solution)/shard_map/ppermute | solution.py:320
  9.8 7.6 %collective-permute-start.3 = (f32[128,256]{1,0:T(8,128)S(1)}, f32[128,256]{1,0:T(8,128)S(1)}, u32[]{:S(2)}, u32[]{:S(2)}) collective-permute-start(f32[128,256]{1,0:T(8,128)S(1)} %get-tuple-element.89), channel_id=1, source_target_pairs={{1,0},{2,1},{3,2},{4,3},{5,4},{6,5},{7,6},{0,7},{9,8},{10,9},{11,1... | collective-permute-start | bytes 393224 | tf_op jit(solution)/shard_map/ppermute | solution.py:320
  18.0 6.6 %collective-permute-start.4 = (f32[64,256]{1,0:T(8,128)S(1)}, f32[64,256]{1,0:T(8,128)S(1)}, u32[]{:S(2)}, u32[]{:S(2)}) collective-permute-start(f32[64,256]{1,0:T(8,128)S(1)} %get-tuple-element.97), channel_id=1, source_target_pairs={{0,1},{1,0},{2,3},{3,2},{4,5},{5,4},{6,7},{7,6},{8,9},{9,8},{10,11... | collective-permute-start | bytes 196616 | tf_op jit(solution)/shard_map/ppermute | solution.py:303
  20.5 4.1 %collective-permute-start.5 = (f32[64,256]{1,0:T(8,128)S(1)}, f32[64,256]{1,0:T(8,128)S(1)}, u32[]{:S(2)}, u32[]{:S(2)}) collective-permute-start(f32[64,256]{1,0:T(8,128)S(1)} %get-tuple-element.98), channel_id=1, source_target_pairs={{0,8},{1,2},{2,1},{3,4},{4,3},{5,6},{6,5},{7,15},{8,0},{9,10},{10,... | collective-permute-start | bytes 196616 | tf_op jit(solution)/shard_map/ppermute | solution.py:302
  20.5 7.6 %collective-permute-start.6 = (f32[64,256]{1,0:T(8,128)S(1)}, f32[64,256]{1,0:T(8,128)S(1)}, u32[]{:S(2)}, u32[]{:S(2)}) collective-permute-start(f32[64,256]{1,0:T(8,128)S(1)} %get-tuple-element.102), channel_id=1, source_target_pairs={{0,1},{1,0},{2,3},{3,2},{4,5},{5,4},{6,7},{7,6},{8,9},{9,8},{10,11... | collective-permute-start | bytes 196616 | tf_op jit(solution)/shard_map/ppermute | solution.py:303
  23.6 4.5 %collective-permute-start.7 = (f32[64,256]{1,0:T(8,128)S(1)}, f32[64,256]{1,0:T(8,128)S(1)}, u32[]{:S(2)}, u32[]{:S(2)}) collective-permute-start(f32[64,256]{1,0:T(8,128)S(1)} %get-tuple-element.103), channel_id=1, source_target_pairs={{0,8},{1,2},{2,1},{3,4},{4,3},{5,6},{6,5},{7,15},{8,0},{9,10},{10,... | collective-permute-start | bytes 196616 | tf_op jit(solution)/shard_map/ppermute | solution.py:302
  25.0 6.9 %collective-permute-start.8 = (f32[64,256]{1,0:T(8,128)S(1)}, f32[64,256]{1,0:T(8,128)S(1)}, u32[]{:S(2)}, u32[]{:S(2)}) collective-permute-start(f32[64,256]{1,0:T(8,128)S(1)} %get-tuple-element.110), channel_id=1, source_target_pairs={{0,1},{1,0},{2,3},{3,2},{4,5},{5,4},{6,7},{7,6},{8,9},{9,8},{10,11... | collective-permute-start | bytes 196616 | tf_op jit(solution)/shard_map/ppermute | solution.py:303
  28.1 3.9 %collective-permute-start.9 = (f32[64,256]{1,0:T(8,128)S(1)}, f32[64,256]{1,0:T(8,128)S(1)}, u32[]{:S(2)}, u32[]{:S(2)}) collective-permute-start(f32[64,256]{1,0:T(8,128)S(1)} %get-tuple-element.111), channel_id=1, source_target_pairs={{0,8},{1,2},{2,1},{3,4},{4,3},{5,6},{6,5},{7,15},{8,0},{9,10},{10,... | collective-permute-start | bytes 196616 | tf_op jit(solution)/shard_map/ppermute | solution.py:302
  28.5 6.8 %collective-permute-start.10 = (f32[64,256]{1,0:T(8,128)S(1)}, f32[64,256]{1,0:T(8,128)S(1)}, u32[]{:S(2)}, u32[]{:S(2)}) collective-permute-start(f32[64,256]{1,0:T(8,128)S(1)} %get-tuple-element.115), channel_id=1, source_target_pairs={{0,1},{1,0},{2,3},{3,2},{4,5},{5,4},{6,7},{7,6},{8,9},{9,8},{10,11... | collective-permute-start | bytes 196616 | tf_op jit(solution)/shard_map/ppermute | solution.py:303
  31.1 4.2 %collective-permute-start.11 = (f32[64,256]{1,0:T(8,128)S(1)}, f32[64,256]{1,0:T(8,128)S(1)}, u32[]{:S(2)}, u32[]{:S(2)}) collective-permute-start(f32[64,256]{1,0:T(8,128)S(1)} %get-tuple-element.116), channel_id=1, source_target_pairs={{0,8},{1,2},{2,1},{3,4},{4,3},{5,6},{6,5},{7,15},{8,0},{9,10},{10,... | collective-permute-start | bytes 196616 | tf_op jit(solution)/shard_map/ppermute | solution.py:302
  32.3 6.4 %collective-permute-start.12 = (f32[64,256]{1,0:T(8,128)S(1)}, f32[64,256]{1,0:T(8,128)S(1)}, u32[]{:S(2)}, u32[]{:S(2)}) collective-permute-start(f32[64,256]{1,0:T(8,128)S(1)} %get-tuple-element.123), channel_id=1, source_target_pairs={{0,1},{1,0},{2,3},{3,2},{4,5},{5,4},{6,7},{7,6},{8,9},{9,8},{10,11... | collective-permute-start | bytes 196616 | tf_op jit(solution)/shard_map/ppermute | solution.py:303
  35.3 3.5 %collective-permute-start.13 = (f32[64,256]{1,0:T(8,128)S(1)}, f32[64,256]{1,0:T(8,128)S(1)}, u32[]{:S(2)}, u32[]{:S(2)}) collective-permute-start(f32[64,256]{1,0:T(8,128)S(1)} %get-tuple-element.124), channel_id=1, source_target_pairs={{0,8},{1,2},{2,1},{3,4},{4,3},{5,6},{6,5},{7,15},{8,0},{9,10},{10,... | collective-permute-start | bytes 196616 | tf_op jit(solution)/shard_map/ppermute | solution.py:302
  35.7 6.2 %collective-permute-start.14 = (f32[64,256]{1,0:T(8,128)S(1)}, f32[64,256]{1,0:T(8,128)S(1)}, u32[]{:S(2)}, u32[]{:S(2)}) collective-permute-start(f32[64,256]{1,0:T(8,128)S(1)} %get-tuple-element.128), channel_id=1, source_target_pairs={{0,1},{1,0},{2,3},{3,2},{4,5},{5,4},{6,7},{7,6},{8,9},{9,8},{10,11... | collective-permute-start | bytes 196616 | tf_op jit(solution)/shard_map/ppermute | solution.py:303
  37.9 4.0 %collective-permute-start.15 = (f32[64,256]{1,0:T(8,128)S(1)}, f32[64,256]{1,0:T(8,128)S(1)}, u32[]{:S(2)}, u32[]{:S(2)}) collective-permute-start(f32[64,256]{1,0:T(8,128)S(1)} %get-tuple-element.129), channel_id=1, source_target_pairs={{0,8},{1,2},{2,1},{3,4},{4,3},{5,6},{6,5},{7,15},{8,0},{9,10},{10,... | collective-permute-start | bytes 196616 | tf_op jit(solution)/shard_map/ppermute | solution.py:302
  39.1 7.0 %collective-permute-start.16 = (f32[64,256]{1,0:T(8,128)S(1)}, f32[64,256]{1,0:T(8,128)S(1)}, u32[]{:S(2)}, u32[]{:S(2)}) collective-permute-start(f32[64,256]{1,0:T(8,128)S(1)} %get-tuple-element.136), channel_id=1, source_target_pairs={{0,1},{1,0},{2,3},{3,2},{4,5},{5,4},{6,7},{7,6},{8,9},{9,8},{10,11... | collective-permute-start | bytes 196616 | tf_op jit(solution)/shard_map/ppermute | solution.py:303
  41.9 4.2 %collective-permute-start.17 = (f32[64,256]{1,0:T(8,128)S(1)}, f32[64,256]{1,0:T(8,128)S(1)}, u32[]{:S(2)}, u32[]{:S(2)}) collective-permute-start(f32[64,256]{1,0:T(8,128)S(1)} %get-tuple-element.137), channel_id=1, source_target_pairs={{0,8},{1,2},{2,1},{3,4},{4,3},{5,6},{6,5},{7,15},{8,0},{9,10},{10,... | collective-permute-start | bytes 196616 | tf_op jit(solution)/shard_map/ppermute | solution.py:302
  42.3 7.3 %collective-permute-start.18 = (f32[64,256]{1,0:T(8,128)S(1)}, f32[64,256]{1,0:T(8,128)S(1)}, u32[]{:S(2)}, u32[]{:S(2)}) collective-permute-start(f32[64,256]{1,0:T(8,128)S(1)} %get-tuple-element.141), channel_id=1, source_target_pairs={{0,1},{1,0},{2,3},{3,2},{4,5},{5,4},{6,7},{7,6},{8,9},{9,8},{10,11... | collective-permute-start | bytes 196616 | tf_op jit(solution)/shard_map/ppermute | solution.py:303
  45.3 4.4 %collective-permute-start.19 = (f32[64,256]{1,0:T(8,128)S(1)}, f32[64,256]{1,0:T(8,128)S(1)}, u32[]{:S(2)}, u32[]{:S(2)}) collective-permute-start(f32[64,256]{1,0:T(8,128)S(1)} %get-tuple-element.142), channel_id=1, source_target_pairs={{0,8},{1,2},{2,1},{3,4},{4,3},{5,6},{6,5},{7,15},{8,0},{9,10},{10,... | collective-permute-start | bytes 196616 | tf_op jit(solution)/shard_map/ppermute | solution.py:302
  46.5 7.0 %collective-permute-start.20 = (f32[64,256]{1,0:T(8,128)S(1)}, f32[64,256]{1,0:T(8,128)S(1)}, u32[]{:S(2)}, u32[]{:S(2)}) collective-permute-start(f32[64,256]{1,0:T(8,128)S(1)} %get-tuple-element.147), channel_id=1, source_target_pairs={{0,1},{1,0},{2,3},{3,2},{4,5},{5,4},{6,7},{7,6},{8,9},{9,8},{10,11... | collective-permute-start | bytes 196616 | tf_op jit(solution)/shard_map/ppermute | solution.py:303
  49.6 3.9 %collective-permute-start.22 = (f32[64,256]{1,0:T(8,128)S(1)}, f32[64,256]{1,0:T(8,128)S(1)}, u32[]{:S(2)}, u32[]{:S(2)}) collective-permute-start(f32[64,256]{1,0:T(8,128)S(1)} %get-tuple-element.149), channel_id=1, source_target_pairs={{0,8},{1,2},{2,1},{3,4},{4,3},{5,6},{6,5},{7,15},{8,0},{9,10},{10,... | collective-permute-start | bytes 196616 | tf_op jit(solution)/shard_map/ppermute | solution.py:302
  50.0 5.3 %collective-permute-start.21 = (f32[64,256]{1,0:T(8,128)S(1)}, f32[64,256]{1,0:T(8,128)S(1)}, u32[]{:S(2)}, u32[]{:S(2)}) collective-permute-start(f32[64,256]{1,0:T(8,128)S(1)} %get-tuple-element.148), channel_id=1, source_target_pairs={{0,1},{1,0},{2,3},{3,2},{4,5},{5,4},{6,7},{7,6},{8,9},{9,8},{10,11... | collective-permute-start | bytes 196616 | tf_op jit(solution)/shard_map/ppermute | solution.py:303
  52.0 3.2 %collective-permute-start.23 = (f32[64,256]{1,0:T(8,128)S(1)}, f32[64,256]{1,0:T(8,128)S(1)}, u32[]{:S(2)}, u32[]{:S(2)}) collective-permute-start(f32[64,256]{1,0:T(8,128)S(1)} %get-tuple-element.150), channel_id=1, source_target_pairs={{0,8},{1,2},{2,1},{3,4},{4,3},{5,6},{6,5},{7,15},{8,0},{9,10},{10,... | collective-permute-start | bytes 196616 | tf_op jit(solution)/shard_map/ppermute | solution.py:302
